TPU v7x, 32 devices: a whole 2x2x4 slice. The times are simulated.
32 devices in a mesh: seq: 16 (over z, y, x), grp: 2 (over core).
Axes of the slice: x: 2, y: 2, z: 4, core: 2. Of those that a mesh axis runs over, the one named last changes fastest.
Arguments:
- query_rows: bfloat16 [2, 2048, 4096], P('grp', 'seq'), may hold values from -6 to 6
- key_rows: bfloat16 [2, 2048, 1024], P('grp', 'seq'), may hold values from -6 to 6
- value_rows: bfloat16 [2, 2048, 1024], P('grp', 'seq'), may hold values from -27 to 27
- doc_of_block: int32 [2, 16], P('grp'), may hold values from 0 to 3, never falling along the last dimension, each value on 1 to 8 neighbouring positions
- expert_ids: int32 [2, 2048, 2], P('grp', 'seq'), may hold values from 0 to 7, as said below
- gate_weights: float32 [2, 2048, 2], P('grp', 'seq'), may hold values from 0.1 to 0.9
- norm_gain: float32 [4096], replicated, may hold values from 0.1 to 1.9
- w_in: bfloat16 [2, 7168, 4096], P(None, ('seq', 'grp')), may hold values from -0.09375 to 0.09375
- w_down: bfloat16 [7168, 4096], P(('seq', 'grp')), may hold values from -0.0625 to 0.0625
Outputs:
- layer_out: bfloat16 [2, 2048, 4096], P('grp', 'seq')
Inputs may be any that keep to these rules, and one draw needn't show every extreme that they name: `expert_ids`: each token names 2 different experts; in each aligned block of 128 tokens along a sequence (the tokens of one device) at most 40 tokens name expert 0, and in every draw some block has exactly 40 such tokens.
All inputs are finite; a program needn't handle non-finite values.
Results may differ from a plain program's by a relative error of at most 0.014.
Values may be sent and summed in bfloat16 or wider, within the bound.
A program may use at most 192 MiB of HBM per device.

v0:
```python
import math

import jax
import jax.numpy as jnp
from jax import lax
from jax.sharding import PartitionSpec as P

QH = 32
KVH = 8
HD = 128
BLK = 128
CAP = 40


EPS = 1e-05
NEG = -1e30


def project_in(gathered, piece):
    return jnp.einsum("rd,khd->krh", gathered, piece, preferred_element_type=jnp.float32)


def activate(gate_up):
    return (jax.nn.silu(gate_up[0]) * gate_up[1]).astype(jnp.bfloat16)


def add_down(hidden, piece):
    return jnp.dot(hidden, piece, preferred_element_type=jnp.float32)


def attend(query_all, key_all, value_all, token_doc, per_dev, kv_local):
    seq_length = query_all.shape[1]
    tile_rows = min(512, seq_length)
    tile_count = seq_length // tile_rows
    per_kv = per_dev // kv_local
    inv_root = 1.0 / math.sqrt(HD)
    query_split = query_all[0].reshape(seq_length, kv_local, per_kv, HD)
    key_split = key_all[0].reshape(seq_length, kv_local, HD)
    value_split = value_all[0].reshape(seq_length, kv_local, HD)
    outputs = []
    for q_index in range(tile_count):
        query_tile = query_split[q_index * tile_rows : (q_index + 1) * tile_rows]
        doc_query = token_doc[q_index * tile_rows : (q_index + 1) * tile_rows]
        allowed_row = doc_query[:, None] == token_doc[None, :]
        scores = (
            jnp.einsum("qkgd,tkd->kgqt", query_tile, key_split, preferred_element_type=jnp.float32)
            * inv_root
        )
        scores = jnp.where(allowed_row, scores, NEG)
        highest = jnp.max(scores, axis=3, keepdims=True)
        weights = jnp.exp(scores - highest)
        denom = jnp.sum(weights, axis=3, keepdims=True)
        mixed = jnp.einsum(
            "kgqt,tkd->qkgd",
            weights.astype(jnp.bfloat16),
            value_split,
            preferred_element_type=jnp.float32,
        )
        mixed = mixed / jnp.transpose(denom, (2, 0, 1, 3))
        outputs.append(mixed.reshape(tile_rows, per_dev * HD).astype(jnp.bfloat16))
    return jnp.concatenate(outputs, axis=0)[None]


def shards(
    query_rows,
    key_rows,
    value_rows,
    doc_of_block,
    expert_ids,
    gate_weights,
    norm_gain,
    w_in,
    w_down,
):
    seq_count = lax.axis_size("seq")
    tok_count = query_rows.shape[1]
    per_dev = QH // seq_count
    repeat_count = max(1, 4 // per_dev)
    kv_local = KVH * repeat_count // seq_count
    key_send = jnp.repeat(key_rows.reshape(1, tok_count, KVH, HD), repeat_count, axis=2).reshape(
        1, tok_count, KVH * repeat_count * HD
    )
    value_send = jnp.repeat(
        value_rows.reshape(1, tok_count, KVH, HD), repeat_count, axis=2
    ).reshape(1, tok_count, KVH * repeat_count * HD)
    query_all, key_all, value_all = (
        lax.all_to_all(query_rows, "seq", split_axis=2, concat_axis=1, tiled=True),
        lax.all_to_all(key_send, "seq", split_axis=2, concat_axis=1, tiled=True),
        lax.all_to_all(value_send, "seq", split_axis=2, concat_axis=1, tiled=True),
    )
    token_doc = jnp.repeat(doc_of_block[0], BLK)
    attended = attend(query_all, key_all, value_all, token_doc, per_dev, kv_local)
    attn_tokens = lax.all_to_all(attended, "seq", split_axis=1, concat_axis=2, tiled=True)
    attn_float = attn_tokens[0].astype(jnp.float32)
    spread = jnp.mean(attn_float * attn_float, axis=-1, keepdims=True)
    normed = (attn_float * lax.rsqrt(spread + EPS) * norm_gain).astype(jnp.bfloat16)
    chosen = expert_ids[0] == 0
    routed = jnp.any(chosen, axis=-1)
    gate_share = jnp.sum(jnp.where(chosen, gate_weights[0], 0.0), axis=-1)
    slot_index = jnp.cumsum(routed.astype(jnp.int32)) - 1
    onehot = (slot_index[None, :] == jnp.arange(CAP, dtype=jnp.int32)[:, None]) & routed[None, :]
    dispatched = jnp.dot(
        onehot.astype(jnp.bfloat16), normed, preferred_element_type=jnp.float32
    ).astype(jnp.bfloat16)
    gathered = lax.all_gather(dispatched, "grp", axis=0, tiled=True)
    gate_up = project_in(gathered, lax.all_gather(w_in, "seq", axis=1, tiled=True))
    hidden = activate(gate_up)
    terms = add_down(hidden, lax.all_gather(w_down, "seq", axis=0, tiled=True))
    returned = lax.psum_scatter(
        terms.astype(jnp.bfloat16), "grp", scatter_dimension=0, tiled=True
    ).astype(jnp.float32)
    picked_rows = jnp.take(returned, jnp.clip(slot_index, 0, CAP - 1), axis=0)
    expert_out = jnp.where(routed[:, None], picked_rows, 0.0)
    layer_out = attn_float + gate_share[:, None] * expert_out
    return layer_out.astype(jnp.bfloat16)[None]


def solution(mesh):
    return jax.shard_map(
        shards,
        mesh=mesh,
        in_specs=(
            P("grp", "seq", None),
            P("grp", "seq", None),
            P("grp", "seq", None),
            P("grp", None),
            P("grp", "seq", None),
            P("grp", "seq", None),
            P(),
            P(None, ("seq", "grp"), None),
            P(("seq", "grp"), None),
        ),
        out_specs=P("grp", "seq", None),
        check_vma=False,
    )
```

profile of v0, /device:TPU:0, one launch (start us, length us, event | category | flops | bytes accessed | tf_op | source)
XLA Modules:
  0.0 1014.7 jit_solution(16004680546261508032)
XLA Ops:
  6.5 0.7 all-gather.3.cloned.1.call-update
  7.3 0.7 all-gather.5.cloned.1.call-update
  8.0 1.1 copy.107
  9.2 8.1 copy.136
  17.4 0.5 broadcast.226
  17.9 11.5 %reduce.20 = bf16[2048,128]{1,0:T(8,128)(2,1)S(1)} reduce(bf16[2048,1,128]{2,1,0:T(2,128)(2,1)S(1)} %bitcast.302, bf16[]{:T(256)} %broadcast.226), dimensions={1}, to_apply=%bitcast.290.reduce_sub_computation | reduce | bytes 1048578
  29.4 0.9 reshape.331
  30.3 8.8 all-to-all-start
  39.1 0.2 copy.108
  39.4 8.1 copy.135
  47.6 11.5 %reduce.19 = bf16[2048,128]{1,0:T(8,128)(2,1)S(1)} reduce(bf16[2048,1,128]{2,1,0:T(2,128)(2,1)S(1)} %bitcast.303, bf16[]{:T(256)} %broadcast.226), dimensions={1}, to_apply=%bitcast.289.reduce_sub_computation | reduce | bytes 1048578
  59.1 0.9 reshape.329
  60.0 4.1 all-to-all-done
  64.1 0.8 copy-done.4
  65.0 9.8 all-to-all-start.2
  74.8 2.8 copy.80
  77.6 22.4 %reduce.21 = bf16[4096,128]{1,0:T(8,128)(2,1)S(1)} reduce(bf16[4096,1,128]{2,1,0:T(2,128)(2,1)S(1)} %bitcast.297, bf16[]{:T(256)} %broadcast.226), dimensions={1}, to_apply=%bitcast.269.reduce_sub_computation | reduce | bytes 2097154
  100.0 1.1 reshape.333
  101.1 7.8 all-to-all-start.1
  109.3 3.8 broadcast_compare_fusion.3
  113.1 0.5 reshape.332
  113.7 1.1 copy.79
  114.8 2.2 reshape.330
  117.1 0.3 copy.85
  117.4 1.0 reshape.324
  118.5 27.8 %all-to-all-done.1 = bf16[16,2,16384]{2,1,0:T(2,128)(2,1)S(1)} async-done(((bf16[16,2,16384]{2,1,0:T(2,128)(2,1)}), bf16[16,2,16384]{2,1,0:T(2,128)(2,1)S(1)}, u32[]{:S(2)}, u32[]{:S(2)}) %all-to-all-start.1) | async-done | bytes 1048608 | tf_op jit(solution)/shard_map/all_to_all | solution.py:87
  146.3 1.0 reshape.334
  147.6 0.1 copy.81
  147.8 3.3 fusion.8
  151.1 2.0 fusion
  153.1 2.6 fusion.51
  155.9 0.1 copy.87
  156.1 2.9 fusion.9
  159.0 2.2 fusion.2
  161.3 2.6 fusion.57
  164.3 2.9 fusion.10
  167.2 2.0 fusion.4
  169.3 3.3 fusion.63
  172.6 1.1 copy.98
  173.9 2.2 fusion.11
  176.1 2.4 fusion.6
  178.6 2.6 fusion.69
  181.4 11.7 %copy.134 = bf16[1,2048,256]{2,0,1:T(2,128)(2,1)S(1)} copy(bf16[1,2048,256]{2,1,0:T(8,128)(2,1)S(1)} %maximum_bitcast_fusion) | data formatting | bytes 2097152 | tf_op jit(solution)/shard_map/broadcast_in_dim | solution.py:61
  193.2 10.6 %reduce.22 = bf16[2048,256]{1,0:T(8,128)(2,1)S(1)} reduce(bf16[2048,1,256]{2,1,0:T(2,128)(2,1)S(1)} %bitcast.295, bf16[]{:T(256)} %broadcast.226), dimensions={1}, to_apply=%bitcast.288.reduce_sub_computation | reduce | bytes 2097154
  203.7 1.1 reshape.335
  204.9 10.8 %all-to-all-start.3 = ((bf16[16,2,16384]{2,1,0:T(2,128)(2,1)}), bf16[16,2,16384]{2,1,0:T(2,128)(2,1)S(1)}, u32[]{:S(2)}, u32[]{:S(2)}) async-start(bf16[16,2,16384]{2,1,0:T(2,128)(2,1)} %reshape.335), calls=%async_computation.3 | async-start | bytes 2097152 | tf_op jit(solution)/shard_map/all_to_all | solution.py:93
  215.8 0.2 reduce-window.4
  216.1 39.1 %all-to-all-done.3 = bf16[16,2,16384]{2,1,0:T(2,128)(2,1)S(1)} async-done(((bf16[16,2,16384]{2,1,0:T(2,128)(2,1)}), bf16[16,2,16384]{2,1,0:T(2,128)(2,1)S(1)}, u32[]{:S(2)}, u32[]{:S(2)}) %all-to-all-start.3) | async-done | bytes 1048608 | tf_op jit(solution)/shard_map/all_to_all | solution.py:93
  255.2 1.0 reshape.336
  256.2 1.2 copy.101
  257.5 1.6 copy.112
  259.1 15.4 %multiply_reduce_fusion = f32[2048]{0:T(1024)S(1)} fusion(bf16[2048,1,256]{2,1,0:T(2,128)(2,1)S(1)} %reshape.336), kind=kLoop, calls=%fused_computation.42 | loop fusion | flops 1570816 | bytes 1056768 | tf_op jit(solution)/shard_map/reduce_sum | solution.py:95
  274.6 0.4 convolution_convert_fusion.1
  274.9 2.3 all_gather.9
  277.2 389.4 %all-gather.3.cloned.1.call-done = bf16[2,3584,4096]{2,1,0:T(8,128)(2,1)} async-done(((bf16[2,224,4096]{2,1,0:T(8,128)(2,1)}), bf16[2,3584,4096]{2,1,0:T(8,128)(2,1)}) %all-gather.3.cloned.1.call-update) | async-done | bytes 58720272 | tf_op jit(solution)/shard_map/all_gather | solution.py:106
  666.6 26.5 %convolution_bitcast_fusion = f32[2,80,3584]{2,1,0:T(8,128)} fusion(bf16[2,3584,4096]{2,1,0:T(8,128)(2,1)} %all-gather.3.cloned.1.call-done, bf16[80,4096]{1,0:T(8,128)(2,1)S(1)} %all_gather.9), kind=kOutput, calls=%fused_computation.21 | convolution fusion | flops 4697620480 | bytes 61669376 | tf_op jit(solution)/shard_map/rd,khd->krh/dot_general | solution.py:20
  693.2 285.6 %all-gather.5.cloned.1.call-done = bf16[3584,4096]{1,0:T(8,128)(2,1)} async-done(((bf16[224,4096]{1,0:T(8,128)(2,1)}), bf16[3584,4096]{1,0:T(8,128)(2,1)}) %all-gather.5.cloned.1.call-update) | async-done | bytes 29360144 | tf_op jit(solution)/shard_map/all_gather | solution.py:108
  978.8 16.0 %convolution_convert_fusion = bf16[80,4096]{1,0:T(8,128)(2,1)} fusion(bf16[3584,4096]{1,0:T(8,128)(2,1)} %all-gather.5.cloned.1.call-done, f32[2,80,3584]{2,1,0:T(8,128)} %convolution_bitcast_fusion), kind=kOutput, calls=%fused_computation.22 | convolution fusion | flops 2350858240 | bytes 32309248 | tf_op jit(solution)/shard_map/dot_general | solution.py:28
  994.9 2.6 copy.133
  997.5 1.8 reshape.310
  999.2 2.1 reduce-scatter.2.cloned.1.call-done
  1001.3 1.0 convert_element_type.131
  1002.3 2.6 gather_fusion
  1004.9 3.1 fusion.31
  (67 shorter events, 2.4 us)
Async XLA Ops:
  6.5 32.6 %copy-start.12 = (bf16[1,128,1024]{2,1,0:T(8,128)(2,1)S(1)}, bf16[1,128,1024]{2,1,0:T(8,128)(2,1)}, u32[]{:S(2)}) copy-start(bf16[1,128,1024]{2,1,0:T(8,128)(2,1)} %param.11) | copy-start | bytes 786436
  6.5 660.1 %all-gather.3.cloned.1.call-start = ((), (), s32[]{:S(2)}) async-start(), calls=%async_computation.5 | async-start | bytes 62390272 | tf_op jit(solution)/shard_map/all_gather | solution.py:106
  7.3 67.5 %copy-start.6 = (bf16[1,128,4096]{2,1,0:T(8,128)(2,1)S(1)}, bf16[1,128,4096]{2,1,0:T(8,128)(2,1)}, u32[]{:S(2)}) copy-start(bf16[1,128,4096]{2,1,0:T(8,128)(2,1)} %param.9) | copy-start | bytes 3145732
  7.3 971.5 %all-gather.5.cloned.1.call-start = ((), (), s32[]{:S(2)}) async-start(), calls=%async_computation.6 | async-start | bytes 31195136 | tf_op jit(solution)/shard_map/all_gather | solution.py:108
  30.3 33.8 %all-to-all-start = ((bf16[16,2,8192]{2,1,0:T(2,128)(2,1)}), bf16[16,2,8192]{2,1,0:T(2,128)(2,1)S(1)}, u32[]{:S(2)}, u32[]{:S(2)}) async-start(bf16[16,2,8192]{2,1,0:T(2,128)(2,1)} %reshape.331), calls=%async_computation | async-start | bytes 1048576 | tf_op jit(solution)/shard_map/all_to_all | solution.py:88
  39.3 69.7 %copy-start.14 = (s32[1,16]{1,0:T(1,128)S(1)}, s32[1,16]{1,0:T(1,128)}, u32[]{:S(2)}) copy-start(s32[1,16]{1,0:T(1,128)} %param.12) | copy-start | bytes 196
  64.1 0.8 copy-start.4
  65.0 36.1 %all-to-all-start.2 = ((bf16[16,2,8192]{2,1,0:T(2,128)(2,1)}), bf16[16,2,8192]{2,1,0:T(2,128)(2,1)}, u32[]{:S(2)}, u32[]{:S(2)}) async-start(bf16[16,2,8192]{2,1,0:T(2,128)(2,1)} %reshape.329), calls=%async_computation.2 | async-start | bytes 1048576 | tf_op jit(solution)/shard_map/all_to_all | solution.py:89
  100.0 13.1 %copy-start.5 = (bf16[16,2,8192]{2,1,0:T(2,128)(2,1)S(1)}, bf16[16,2,8192]{2,1,0:T(2,128)(2,1)}, u32[]{:S(2)}) copy-start(bf16[16,2,8192]{2,1,0:T(2,128)(2,1)} %copy-done.4) | copy-start | bytes 1572868
  101.1 45.1 %all-to-all-start.1 = ((bf16[16,2,16384]{2,1,0:T(2,128)(2,1)}), bf16[16,2,16384]{2,1,0:T(2,128)(2,1)S(1)}, u32[]{:S(2)}, u32[]{:S(2)}) async-start(bf16[16,2,16384]{2,1,0:T(2,128)(2,1)} %reshape.333), calls=%async_computation.1 | async-start | bytes 2097152 | tf_op jit(solution)/shard_map/all_to_all | solution.py:87
  147.4 3.6 copy-start.3
  147.8 5.3 copy-start.8
  153.1 3.0 copy-start.2
  156.1 5.2 copy-start.9
  161.3 3.0 copy-start.1
  164.3 5.0 copy-start.10
  169.2 4.6 copy-start
  169.2 4.6 copy-start.7
  173.9 4.6 copy-start.11
  181.2 34.5 %copy-start.15 = (s32[1,128,2]{1,2,0:T(2,128)S(1)}, s32[1,128,2]{1,2,0:T(2,128)}, u32[]{:S(2)}) copy-start(s32[1,128,2]{1,2,0:T(2,128)} %param.13) | copy-start | bytes 3076
  204.9 69.7 %copy-start.13 = (f32[4096]{0:T(1024)S(1)}, f32[4096]{0:T(1024)}, u32[]{:S(2)}) copy-start(f32[4096]{0:T(1024)} %param.15) | copy-start | bytes 49156
  204.9 50.3 %all-to-all-start.3 = ((bf16[16,2,16384]{2,1,0:T(2,128)(2,1)}), bf16[16,2,16384]{2,1,0:T(2,128)(2,1)S(1)}, u32[]{:S(2)}, u32[]{:S(2)}) async-start(bf16[16,2,16384]{2,1,0:T(2,128)(2,1)} %reshape.335), calls=%async_computation.3 | async-start | bytes 2097152 | tf_op jit(solution)/shard_map/all_to_all | solution.py:93
  215.6 785.7 %reduce-scatter.2.cloned.1.call-start = ((), (), s32[]{:S(2)}) async-start(), calls=%async_computation.7 | async-start | bytes 983040 | tf_op jit(solution)/shard_map/reduce_scatter | solution.py:109
  693.2 301.7 %copy-start.16 = (f32[1,128,2]{1,2,0:T(2,128)S(1)}, f32[1,128,2]{1,2,0:T(2,128)}, u32[]{:S(2)}) copy-start(f32[1,128,2]{1,2,0:T(2,128)} %param.14) | copy-start | bytes 3076
Sparse Core Ops, SparseCore 0:
  10.1 656.5 all-gather.2
  669.3 309.3 all-gather.4
  995.0 6.2 reduce-scatter.1
where the time goes:
time: 1020 us; the launch traced here: 1010 us
  waiting for transfers between devices  749 us (73%)
  other arithmetic  88.4 us (9%)
  matrix products  65.5 us (6%)
  local copies, waits for them, and re-layouts  58 us (6%)
  starting transfers between devices  37.3 us (4%)
  between operations  13.9 us (1%)
    all_gather x1, waiting for transfers between devices, shards(): lax.all_gather(w_in, 'seq', axis=1, tiled=True)  389 us
    all_gather x1, waiting for transfers between devices, shards(): terms = add_down(hidden, lax.all_gather(w_down, 'seq', axis=0, tiled=True))  286 us
    unnamed x4, other arithmetic  56 us
    all_to_all x1, waiting for transfers between devices, shards(): lax.all_to_all(attended, 'seq', split_axis=1, concat_axis=2, tiled=True)  39.1 us
    all_to_all x1, waiting for transfers between devices, shards(): lax.all_to_all(query_rows, 'seq', split_axis=2, concat_axis=1, tiled=True)  27.8 us
    dot_general x1, matrix products, project_in(): jnp.einsum('rd,khd->krh', gathered, piece, preferred_element_type=jnp.flo...  26.5 us
  transfers between devices with their start and end apart: 7, of which 6 were waited for; matrix products, arithmetic and copies ran while one was open for 19% of the time, Pallas kernels for 0%

commit v1 on v0

--- a/solution.py
+++ b/solution.py
@@ -97,20 +97,28 @@
     chosen = expert_ids[0] == 0
     routed = jnp.any(chosen, axis=-1)
     gate_share = jnp.sum(jnp.where(chosen, gate_weights[0], 0.0), axis=-1)
-    slot_index = jnp.cumsum(routed.astype(jnp.int32)) - 1
+    position = jnp.arange(tok_count, dtype=jnp.int32)
+    earlier = (position[None, :] <= position[:, None]) & routed[None, :]
+    slot_index = jnp.sum(earlier.astype(jnp.int32), axis=1) - 1
     onehot = (slot_index[None, :] == jnp.arange(CAP, dtype=jnp.int32)[:, None]) & routed[None, :]
     dispatched = jnp.dot(
         onehot.astype(jnp.bfloat16), normed, preferred_element_type=jnp.float32
     ).astype(jnp.bfloat16)
-    gathered = lax.all_gather(dispatched, "grp", axis=0, tiled=True)
-    gate_up = project_in(gathered, lax.all_gather(w_in, "seq", axis=1, tiled=True))
+    w_in_pair = lax.all_gather(w_in, "grp", axis=1, tiled=True)
+    w_down_pair = lax.all_gather(w_down, "grp", axis=0, tiled=True)
+    gathered = lax.all_gather(dispatched, "seq", axis=0, tiled=True)
+    gate_up = project_in(gathered, w_in_pair)
     hidden = activate(gate_up)
-    terms = add_down(hidden, lax.all_gather(w_down, "seq", axis=0, tiled=True))
+    terms = add_down(hidden, w_down_pair)
     returned = lax.psum_scatter(
-        terms.astype(jnp.bfloat16), "grp", scatter_dimension=0, tiled=True
-    ).astype(jnp.float32)
-    picked_rows = jnp.take(returned, jnp.clip(slot_index, 0, CAP - 1), axis=0)
-    expert_out = jnp.where(routed[:, None], picked_rows, 0.0)
+        terms.astype(jnp.bfloat16), "seq", scatter_dimension=0, tiled=True
+    )
+    expert_out = lax.dot_general(
+        onehot.astype(jnp.bfloat16),
+        returned,
+        (((0,), (0,)), ((), ())),
+        preferred_element_type=jnp.float32,
+    )
     layer_out = attn_float + gate_share[:, None] * expert_out
     return layer_out.astype(jnp.bfloat16)[None]
 

time: 1020 us -> 471 us (0.46)
  waiting for transfers between devices: 749 us -> 241 us
  matrix products: 65.5 us -> 43.6 us
    all_gather x2 -> x3, waiting for transfers between devices: 675 us -> 86.9 us  [the longest x1 84.9 us: shards(): gathered = lax.all_gather(dispatched, 'seq', axis=0, tiled=True)]
    reduce_scatter x1, waiting for transfers between devices: 2.07 us -> 117 us  [shards(): lax.psum_scatter(terms.astype(jnp.bfloat16), 'seq', scatter_dimension=0,...]
    all_to_all x1, waiting for transfers between devices: 39.1 us -> 22.7 us  [shards(): lax.all_to_all(attended, 'seq', split_axis=1, concat_axis=2, tiled=True)]
    dot_general x1, matrix products: 26.5 us -> 11 us  [project_in(): jnp.einsum('rd,khd->krh', gathered, piece, preferred_element_type=jnp.flo...]
    all_to_all x1, waiting for transfers between devices: 27.8 us -> 13.2 us  [shards(): lax.all_to_all(query_rows, 'seq', split_axis=2, concat_axis=1, tiled=True)]
  transfers between devices with their start and end apart: 7 -> 8, of which waited for: 6 -> 5; matrix products, arithmetic and copies ran while one was open for 19% -> 31% of each run, Pallas kernels for 0% -> 0%
where the time goes in v1:
time: 471 us; the launch traced here: 464 us
  waiting for transfers between devices  241 us (51%)
  other arithmetic  84.8 us (18%)
  local copies, waits for them, and re-layouts  51.3 us (11%)
  matrix products  43.6 us (9%)
  starting transfers between devices  29.1 us (6%)
  between operations  14.2 us (3%)
    reduce_scatter x1, waiting for transfers between devices, shards(): lax.psum_scatter(terms.astype(jnp.bfloat16), 'seq', scatter_dimension=0,...  117 us
    all_gather x1, waiting for transfers between devices, shards(): gathered = lax.all_gather(dispatched, 'seq', axis=0, tiled=True)  84.9 us
    unnamed x4, other arithmetic  55.9 us
    all_to_all x1, waiting for transfers between devices, shards(): lax.all_to_all(attended, 'seq', split_axis=1, concat_axis=2, tiled=True)  22.7 us
    reduce_sum x2, other arithmetic, shards(): spread = jnp.mean(attn_float * attn_float, axis=-1, keepdims=True)  16.5 us
    unnamed x46, local copies, waits for them, and re-layouts  15.4 us
    all_to_all x1, waiting for transfers between devices, shards(): lax.all_to_all(query_rows, 'seq', split_axis=2, concat_axis=1, tiled=True)  13.2 us
    broadcast_in_dim x1, local copies, waits for them, and re-layouts, attend(): return jnp.concatenate(outputs, axis=0)[None]  11.7 us
  transfers between devices with their start and end apart: 8, of which 5 were waited for; matrix products, arithmetic and copies ran while one was open for 31% of the time, Pallas kernels for 0%

profile of v1, /device:TPU:0, one launch (start us, length us, event | category | flops | bytes accessed | tf_op | source)
XLA Modules:
  0.0 463.7 jit_solution(14019686417689351697)
XLA Ops:
  6.5 1.2 copy.102
  7.9 8.1 %copy.129 = bf16[1,128,2048]{1,0,2:T(2,128)(2,1)S(1)} copy(bf16[1,128,2048]{1,2,0:T(8,128)(2,1)S(1)} %bitcast.292) | data formatting | bytes 1048576 | tf_op jit(solution)/shard_map/broadcast_in_dim | solution.py:80
  16.0 0.5 broadcast.108
  16.5 11.5 %reduce.16 = bf16[2048,128]{1,0:T(8,128)(2,1)S(1)} reduce(bf16[2048,1,128]{2,1,0:T(2,128)(2,1)S(1)} %bitcast.290, bf16[]{:T(256)} %broadcast.108), dimensions={1}, to_apply=%bitcast.279.reduce_sub_computation | reduce | bytes 1048578
  28.0 0.9 reshape.196
  28.9 8.5 %all-to-all-start = ((bf16[16,2,8192]{2,1,0:T(2,128)(2,1)}), bf16[16,2,8192]{2,1,0:T(2,128)(2,1)S(1)}, u32[]{:S(2)}, u32[]{:S(2)}) async-start(bf16[16,2,8192]{2,1,0:T(2,128)(2,1)} %reshape.196), calls=%async_computation | async-start | bytes 1048576 | tf_op jit(solution)/shard_map/all_to_all | solution.py:88
  37.5 1.1 copy.103
  38.7 8.1 %copy.128 = bf16[1,128,2048]{1,0,2:T(2,128)(2,1)S(1)} copy(bf16[1,128,2048]{1,2,0:T(8,128)(2,1)S(1)} %bitcast.293) | data formatting | bytes 1048576 | tf_op jit(solution)/shard_map/broadcast_in_dim | solution.py:83
  46.9 11.5 %reduce.15 = bf16[2048,128]{1,0:T(8,128)(2,1)S(1)} reduce(bf16[2048,1,128]{2,1,0:T(2,128)(2,1)S(1)} %bitcast.291, bf16[]{:T(256)} %broadcast.108), dimensions={1}, to_apply=%bitcast.278.reduce_sub_computation | reduce | bytes 1048578
  58.4 0.9 reshape.194
  59.3 0.8 copy-done.5
  60.1 7.1 %all-to-all-start.2 = ((bf16[16,2,8192]{2,1,0:T(2,128)(2,1)}), bf16[16,2,8192]{2,1,0:T(2,128)(2,1)}, u32[]{:S(2)}, u32[]{:S(2)}) async-start(bf16[16,2,8192]{2,1,0:T(2,128)(2,1)} %reshape.194), calls=%async_computation.2 | async-start | bytes 1048576 | tf_op jit(solution)/shard_map/all_to_all | solution.py:89
  67.2 2.8 copy.76
  70.0 22.4 %reduce.17 = bf16[4096,128]{1,0:T(8,128)(2,1)S(1)} reduce(bf16[4096,1,128]{2,1,0:T(2,128)(2,1)S(1)} %bitcast.285, bf16[]{:T(256)} %broadcast.108), dimensions={1}, to_apply=%bitcast.258.reduce_sub_computation | reduce | bytes 2097154
  92.4 1.1 reshape.198
  93.5 7.0 %all-to-all-start.1 = ((bf16[16,2,16384]{2,1,0:T(2,128)(2,1)}), bf16[16,2,16384]{2,1,0:T(2,128)(2,1)S(1)}, u32[]{:S(2)}, u32[]{:S(2)}) async-start(bf16[16,2,16384]{2,1,0:T(2,128)(2,1)} %reshape.198), calls=%async_computation.1 | async-start | bytes 2097152 | tf_op jit(solution)/shard_map/all_to_all | solution.py:87
  100.5 0.4 all-gather.6.cloned.1.call-start
  100.9 0.3 all-gather.6.cloned.1.call-update
  101.5 3.8 broadcast_compare_fusion.3
  105.3 0.5 reshape.197
  105.9 1.0 copy.75
  107.0 2.2 reshape.195
  109.3 0.3 copy.81
  109.6 1.0 reshape.191
  110.6 13.2 %all-to-all-done.1 = bf16[16,2,16384]{2,1,0:T(2,128)(2,1)S(1)} async-done(((bf16[16,2,16384]{2,1,0:T(2,128)(2,1)}), bf16[16,2,16384]{2,1,0:T(2,128)(2,1)S(1)}, u32[]{:S(2)}, u32[]{:S(2)}) %all-to-all-start.1) | async-done | bytes 1048608 | tf_op jit(solution)/shard_map/all_to_all | solution.py:87
  123.8 1.0 reshape.199
  124.9 0.1 copy.106
  125.1 0.1 copy.77
  125.3 0.1 copy.83
  125.6 3.3 fusion.8
  128.9 2.0 fusion
  130.9 2.6 fusion.55
  133.5 2.2 fusion.9
  135.8 2.2 fusion.2
  137.9 2.6 fusion.61
  140.6 0.1 copy.92
  140.7 0.1 copy.93
  140.8 0.1 copy.86
  141.1 2.2 fusion.10
  143.3 2.0 fusion.4
  145.3 2.6 fusion.67
  147.9 0.1 copy.94
  148.1 0.1 copy.89
  148.3 2.9 fusion.11
  151.3 2.2 fusion.6
  153.5 2.6 fusion.73
  156.3 11.7 %copy.127 = bf16[1,2048,256]{2,0,1:T(2,128)(2,1)S(1)} copy(bf16[1,2048,256]{2,1,0:T(8,128)(2,1)S(1)} %maximum_bitcast_fusion) | data formatting | bytes 2097152 | tf_op jit(solution)/shard_map/broadcast_in_dim | solution.py:61
  168.1 10.6 %reduce.18 = bf16[2048,256]{1,0:T(8,128)(2,1)S(1)} reduce(bf16[2048,1,256]{2,1,0:T(2,128)(2,1)S(1)} %bitcast.284, bf16[]{:T(256)} %broadcast.108), dimensions={1}, to_apply=%bitcast.277.reduce_sub_computation | reduce | bytes 2097154
  178.7 1.1 reshape.200
  179.8 6.0 %all-to-all-start.3 = ((bf16[16,2,16384]{2,1,0:T(2,128)(2,1)}), bf16[16,2,16384]{2,1,0:T(2,128)(2,1)S(1)}, u32[]{:S(2)}, u32[]{:S(2)}) async-start(bf16[16,2,16384]{2,1,0:T(2,128)(2,1)} %reshape.200), calls=%async_computation.3 | async-start | bytes 2097152 | tf_op jit(solution)/shard_map/all_to_all | solution.py:93
  186.0 22.7 %all-to-all-done.3 = bf16[16,2,16384]{2,1,0:T(2,128)(2,1)S(1)} async-done(((bf16[16,2,16384]{2,1,0:T(2,128)(2,1)}), bf16[16,2,16384]{2,1,0:T(2,128)(2,1)S(1)}, u32[]{:S(2)}, u32[]{:S(2)}) %all-to-all-start.3) | async-done | bytes 1048608 | tf_op jit(solution)/shard_map/all_to_all | solution.py:93
  208.7 1.3 reshape.201
  210.0 1.2 copy.97
  211.2 0.1 copy-done
  211.4 1.6 copy.107
  213.0 16.4 %multiply_reduce_fusion = f32[2048]{0:T(1024)S(1)} fusion(bf16[2048,1,256]{2,1,0:T(2,128)(2,1)} %copy-done), kind=kLoop, calls=%fused_computation.41 | loop fusion | flops 1570816 | bytes 1056768 | tf_op jit(solution)/shard_map/reduce_sum | solution.py:95
  229.5 1.1 convolution_convert_fusion.1
  230.7 0.7 all-gather.8.cloned.1.call-update
  231.4 84.9 %all-gather.4.cloned.1.call-done = bf16[640,4096]{1,0:T(8,128)(2,1)} async-done(((bf16[40,4096]{1,0:T(8,128)(2,1)}), bf16[640,4096]{1,0:T(8,128)(2,1)}) %all-gather.4.cloned.1.call-update) | async-done | bytes 5242896 | tf_op jit(solution)/shard_map/all_gather | solution.py:109
  316.3 11.0 %fusion.33 = f32[2,640,448]{1,2,0:T(8,128)} fusion(bf16[2,448,4096]{2,1,0:T(8,128)(2,1)} %all-gather.6.cloned.1.call-done, bf16[640,4096]{1,0:T(8,128)(2,1)} %all-gather.4.cloned.1.call-done), kind=kOutput, calls=%fused_computation.46 | convolution fusion | flops 4697620480 | bytes 14876672 | tf_op jit(solution)/shard_map/rd,khd->krh/dot_general | solution.py:20
  327.4 2.0 all-gather.8.cloned.1.call-done
  329.4 8.0 %convolution_convert_fusion = bf16[640,4096]{1,0:T(8,128)(2,1)} fusion(bf16[448,4096]{1,0:T(8,128)(2,1)} %all-gather.8.cloned.1.call-done, f32[2,640,448]{1,2,0:T(8,128)} %fusion.33), kind=kOutput, calls=%fused_computation.20 | convolution fusion | flops 2353152000 | bytes 11206656 | tf_op jit(solution)/shard_map/dot_general | solution.py:28
  337.4 116.8 %reduce-scatter.2.cloned.1.call-done = bf16[40,4096]{1,0:T(8,128)(2,1)} async-done(((bf16[640,4096]{1,0:T(8,128)(2,1)}), bf16[40,4096]{1,0:T(8,128)(2,1)}) %reduce-scatter.2.cloned.1.call-update) | async-done | bytes 327696 | tf_op jit(solution)/shard_map/reduce_scatter | solution.py:113
  454.2 2.4 fusion.16
  (59 shorter events, 1.6 us)
Async XLA Ops:
  6.5 60.6 %copy-start.7 = (bf16[1,128,4096]{2,1,0:T(8,128)(2,1)S(1)}, bf16[1,128,4096]{2,1,0:T(8,128)(2,1)}, u32[]{:S(2)}) copy-start(bf16[1,128,4096]{2,1,0:T(8,128)(2,1)} %param.9) | copy-start | bytes 3145732
  28.9 30.3 %all-to-all-start = ((bf16[16,2,8192]{2,1,0:T(2,128)(2,1)}), bf16[16,2,8192]{2,1,0:T(2,128)(2,1)S(1)}, u32[]{:S(2)}, u32[]{:S(2)}) async-start(bf16[16,2,8192]{2,1,0:T(2,128)(2,1)} %reshape.196), calls=%async_computation | async-start | bytes 1048576 | tf_op jit(solution)/shard_map/all_to_all | solution.py:88
  58.3 42.9 %copy-start.13 = (s32[1,16]{1,0:T(1,128)S(1)}, s32[1,16]{1,0:T(1,128)}, u32[]{:S(2)}) copy-start(s32[1,16]{1,0:T(1,128)} %param.12) | copy-start | bytes 196
  59.3 0.8 copy-start.5
  60.1 33.4 %all-to-all-start.2 = ((bf16[16,2,8192]{2,1,0:T(2,128)(2,1)}), bf16[16,2,8192]{2,1,0:T(2,128)(2,1)}, u32[]{:S(2)}, u32[]{:S(2)}) async-start(bf16[16,2,8192]{2,1,0:T(2,128)(2,1)} %reshape.194), calls=%async_computation.2 | async-start | bytes 1048576 | tf_op jit(solution)/shard_map/all_to_all | solution.py:89
  93.5 11.9 %copy-start.6 = (bf16[16,2,8192]{2,1,0:T(2,128)(2,1)S(1)}, bf16[16,2,8192]{2,1,0:T(2,128)(2,1)}, u32[]{:S(2)}) copy-start(bf16[16,2,8192]{2,1,0:T(2,128)(2,1)} %copy-done.5) | copy-start | bytes 1572868
  93.5 30.3 %all-to-all-start.1 = ((bf16[16,2,16384]{2,1,0:T(2,128)(2,1)}), bf16[16,2,16384]{2,1,0:T(2,128)(2,1)S(1)}, u32[]{:S(2)}, u32[]{:S(2)}) async-start(bf16[16,2,16384]{2,1,0:T(2,128)(2,1)} %reshape.198), calls=%async_computation.1 | async-start | bytes 2097152 | tf_op jit(solution)/shard_map/all_to_all | solution.py:87
  100.5 130.9 %all-gather.6.cloned.1.call-start = ((), (), s32[]{:S(2)}) async-start(), calls=%async_computation.6 | async-start | bytes 11010048 | tf_op jit(solution)/shard_map/all_gather | solution.py:107
  125.0 3.8 copy-start.4
  125.6 5.3 %copy-start.9 = (bf16[2048,128,1]{0,1,2:T(8,128)(2,1)S(1)}, bf16[2048,128,1]{0,1,2:T(8,128)(2,1)}, u32[]{:S(2)}) copy-start(bf16[2048,128,1]{0,1,2:T(8,128)(2,1)} %reshape.191) | copy-start | bytes 1572868
  130.9 2.6 copy-start.3
  130.9 2.6 copy-start.8
  137.9 3.1 copy-start.2
  141.1 4.2 copy-start.10
  145.3 3.0 copy-start.1
  148.3 5.2 %copy-start.11 = (bf16[2048,128,1]{0,1,2:T(8,128)(2,1)S(1)}, bf16[2048,128,1]{0,1,2:T(8,128)(2,1)}, u32[]{:S(2)}) copy-start(bf16[2048,128,1]{0,1,2:T(8,128)(2,1)} %reshape.191) | copy-start | bytes 1572868
  156.1 29.7 %copy-start.14 = (s32[1,128,2]{1,2,0:T(2,128)S(1)}, s32[1,128,2]{1,2,0:T(2,128)}, u32[]{:S(2)}) copy-start(s32[1,128,2]{1,2,0:T(2,128)} %param.13) | copy-start | bytes 3076
  179.8 49.7 %copy-start.12 = (f32[4096]{0:T(1024)S(1)}, f32[4096]{0:T(1024)}, u32[]{:S(2)}) copy-start(f32[4096]{0:T(1024)} %param.15) | copy-start | bytes 49156
  179.8 28.9 %all-to-all-start.3 = ((bf16[16,2,16384]{2,1,0:T(2,128)(2,1)}), bf16[16,2,16384]{2,1,0:T(2,128)(2,1)S(1)}, u32[]{:S(2)}, u32[]{:S(2)}) async-start(bf16[16,2,16384]{2,1,0:T(2,128)(2,1)} %reshape.200), calls=%async_computation.3 | async-start | bytes 2097152 | tf_op jit(solution)/shard_map/all_to_all | solution.py:93
  185.8 130.6 %all-gather.4.cloned.1.call-start = ((), (), s32[]{:S(2)}) async-start(), calls=%async_computation.5 | async-start | bytes 5570560 | tf_op jit(solution)/shard_map/all_gather | solution.py:109
  210.0 1.4 copy-start
  230.6 98.7 %all-gather.8.cloned.1.call-start = ((), (), s32[]{:S(2)}) async-start(), calls=%async_computation.7 | async-start | bytes 5505024 | tf_op jit(solution)/shard_map/all_gather | solution.py:108
  231.4 222.9 %reduce-scatter.2.cloned.1.call-start = ((), (), s32[]{:S(2)}) async-start(), calls=%async_computation.8 | async-start | bytes 5570560 | tf_op jit(solution)/shard_map/reduce_scatter | solution.py:113
  327.4 10.1 %copy-start.15 = (f32[1,128,2]{1,2,0:T(2,128)S(1)}, f32[1,128,2]{1,2,0:T(2,128)}, u32[]{:S(2)}) copy-start(f32[1,128,2]{1,2,0:T(2,128)} %param.14) | copy-start | bytes 3076
Sparse Core Ops, SparseCore 0:
  102.8 19.5 all-gather.5
  230.7 85.5 all-gather.3
  317.9 11.4 all-gather.7
  337.5 116.6 reduce-scatter.1

commit v2 on v1

v2 whole, which is shorter than its diff:
```python
import functools
import math

import jax
import jax.numpy as jnp
from jax import lax
from jax.experimental import pallas as pl
from jax.experimental.pallas import tpu as pltpu
from jax.sharding import PartitionSpec as P

QH = 32
KVH = 8
HD = 128
BLK = 128
CAP = 40


DOC_MOST = 8
TEAM = 4

EPS = 1e-05
NEG = -1e30


def greet_all(n, me):
    barrier = pltpu.get_barrier_semaphore()
    for d in range(1, n):
        pl.semaphore_signal(
            barrier,
            inc=1,
            device_id={"seq": lax.rem(me + d, n)},
            device_id_type=pl.DeviceIdType.MESH,
        )
    pl.semaphore_wait(barrier, n - 1)


def greet_team(base, j):
    barrier = pltpu.get_barrier_semaphore()
    for d in range(1, TEAM):
        pl.semaphore_signal(
            barrier,
            inc=1,
            device_id={"seq": base + lax.rem(j + d, TEAM)},
            device_id_type=pl.DeviceIdType.MESH,
        )
    pl.semaphore_wait(barrier, TEAM - 1)


def span(index, size):
    return pl.ds(pl.multiple_of(index * size, size), size)


def spread_kernel(n, q_ref, k_ref, v_ref, qo_ref, ko_ref, vo_ref, *sems):
    qs, qr, ks, kr, vs, vr, own = sems
    me = lax.axis_index("seq")
    team = me // TEAM
    j = lax.rem(me, TEAM)
    tok = q_ref.shape[0]
    qw, kw = qo_ref.shape[1], ko_ref.shape[1]
    greet_all(n, me)

    def q_copy(d):
        to = lax.rem(j + d, TEAM)
        return pltpu.make_async_remote_copy(
            src_ref=q_ref.at[:, span(to, qw)],
            dst_ref=qo_ref.at[span(j, tok), :],
            send_sem=qs.at[d],
            recv_sem=qr.at[d],
            device_id={"seq": team * TEAM + to},
            device_id_type=pl.DeviceIdType.MESH,
        )

    def kv_copy(d, src, dst, send, recv):
        to = lax.rem(me + d, n)
        return pltpu.make_async_remote_copy(
            src_ref=src.at[:, span(lax.rem(to, TEAM), kw)],
            dst_ref=dst.at[span(me, tok), :],
            send_sem=send.at[d],
            recv_sem=recv.at[d],
            device_id={"seq": to},
            device_id_type=pl.DeviceIdType.MESH,
        )

    def kv_pair(d):
        return kv_copy(d, k_ref, ko_ref, ks, kr), kv_copy(d, v_ref, vo_ref, vs, vr)

    def wanted(source, team_to):
        reach = DOC_MOST - 1
        first = team_to * TEAM
        return (first - source <= reach) & (source - first <= reach + TEAM - 1)

    mine = [
        pltpu.make_async_copy(q_ref.at[:, span(j, qw)], qo_ref.at[span(j, tok), :], own.at[0]),
        pltpu.make_async_copy(k_ref.at[:, span(j, kw)], ko_ref.at[span(me, tok), :], own.at[1]),
        pltpu.make_async_copy(v_ref.at[:, span(j, kw)], vo_ref.at[span(me, tok), :], own.at[2]),
    ]
    order = sorted(range(1, n), key=lambda d: -min(d, n - d))

    def start(d):
        @pl.when(wanted(me, lax.rem(me + d, n) // TEAM))
        def _():
            for copy in kv_pair(d):
                copy.start()

    for d in order[:4]:
        start(d)
    for d in range(1, TEAM):
        q_copy(d).start()
    for d in order[4:]:
        start(d)
    for copy in mine:
        copy.start()
    for copy in mine:
        copy.wait()
    for d in range(1, TEAM):
        q_copy(d).wait()
    for d in order:

        @pl.when(wanted(me, lax.rem(me + d, n) // TEAM))
        def _():
            for copy in kv_pair(d):
                copy.wait_send()

        @pl.when(wanted(lax.rem(me - d + n, n), team))
        def _():
            for copy in kv_pair(d):
                copy.wait_recv()


def spread(n, q, k, v):
    tok = q.shape[0]
    any_spec = pl.BlockSpec(memory_space=pl.ANY)
    kv = jax.ShapeDtypeStruct((n * tok, KVH * HD // TEAM), jnp.bfloat16)
    dma = pltpu.SemaphoreType.DMA
    return pl.pallas_call(
        functools.partial(spread_kernel, n),
        out_shape=(jax.ShapeDtypeStruct((TEAM * tok, QH * HD // TEAM), jnp.bfloat16), kv, kv),
        in_specs=[any_spec] * 3,
        out_specs=(any_spec,) * 3,
        scratch_shapes=[dma((TEAM,))] * 2 + [dma((n,))] * 4 + [dma((3,))],
        compiler_params=pltpu.CompilerParams(collective_id=0, has_side_effects=True),
        name="spread",
    )(q, k, v)


def attend_kernel(start_ref, low_ref, high_ref, q_ref, k_ref, v_ref, o_ref):
    qb = pl.program_id(1)
    width = DOC_MOST * BLK
    start = start_ref[qb]
    low = (low_ref[qb] - start) * BLK
    high = (high_ref[qb] - start + 1) * BLK
    rows = pl.ds(pl.multiple_of(start * BLK, BLK), width)
    keys = k_ref[rows, :]
    row_at = lax.broadcasted_iota(jnp.int32, (width, HD), 0)
    values = v_ref[rows, :]
    values = jnp.where((row_at >= low) & (row_at < high), values, jnp.zeros_like(values))
    at = lax.broadcasted_iota(jnp.int32, (1, width), 1)
    seen = (at >= low) & (at < high)
    for h in range(QH // KVH):
        scores = lax.dot_general(
            q_ref[:, h * HD : (h + 1) * HD],
            keys,
            (((1,), (1,)), ((), ())),
            preferred_element_type=jnp.float32,
        ) * (1.0 / math.sqrt(HD))
        scores = jnp.where(seen, scores, NEG)
        weights = jnp.exp(scores - jnp.max(scores, axis=1, keepdims=True))
        denom = jnp.sum(weights, axis=1, keepdims=True)
        mixed = jnp.dot(weights.astype(jnp.bfloat16), values, preferred_element_type=jnp.float32)
        o_ref[:, h * HD : (h + 1) * HD] = (mixed / denom).astype(jnp.bfloat16)


def attend(start, low, high, q, k, v):
    kv_here = k.shape[1] // HD
    group = QH // KVH * HD
    length = k.shape[0]
    return pl.pallas_call(
        attend_kernel,
        out_shape=jax.ShapeDtypeStruct(q.shape, jnp.bfloat16),
        grid_spec=pltpu.PrefetchScalarGridSpec(
            num_scalar_prefetch=3,
            grid=(kv_here, q.shape[0] // BLK),
            in_specs=[
                pl.BlockSpec((BLK, group), lambda h, b, *_: (b, h)),
                pl.BlockSpec((length, HD), lambda h, b, *_: (0, h)),
                pl.BlockSpec((length, HD), lambda h, b, *_: (0, h)),
            ],
            out_specs=pl.BlockSpec((BLK, group), lambda h, b, *_: (b, h)),
        ),
        compiler_params=pltpu.CompilerParams(vmem_limit_bytes=40 * 2**20),
        name="attend",
    )(start, low, high, q, k, v)


def collect_kernel(a_ref, o_ref, send, recv, own):
    me = lax.axis_index("seq")
    base = me // TEAM * TEAM
    j = lax.rem(me, TEAM)
    tok, width = o_ref.shape[0], a_ref.shape[1]
    greet_team(base, j)

    def copy(d):
        to = lax.rem(j + d, TEAM)
        return pltpu.make_async_remote_copy(
            src_ref=a_ref.at[span(to, tok), :],
            dst_ref=o_ref.at[:, span(j, width)],
            send_sem=send.at[d],
            recv_sem=recv.at[d],
            device_id={"seq": base + to},
            device_id_type=pl.DeviceIdType.MESH,
        )

    for d in range(1, TEAM):
        copy(d).start()
    mine = pltpu.make_async_copy(
        a_ref.at[span(j, tok), :], o_ref.at[:, span(j, width)], own.at[0]
    )
    mine.start()
    mine.wait()
    for d in range(1, TEAM):
        copy(d).wait()


def collect(attended):
    any_spec = pl.BlockSpec(memory_space=pl.ANY)
    dma = pltpu.SemaphoreType.DMA
    return pl.pallas_call(
        collect_kernel,
        out_shape=jax.ShapeDtypeStruct((attended.shape[0] // TEAM, QH * HD), jnp.bfloat16),
        in_specs=[any_spec],
        out_specs=any_spec,
        scratch_shapes=[dma((TEAM,)), dma((TEAM,)), dma((1,))],
        compiler_params=pltpu.CompilerParams(collective_id=1, has_side_effects=True),
        name="collect",
    )(attended)


def project_in(gathered, piece):
    return jnp.einsum("rd,khd->krh", gathered, piece, preferred_element_type=jnp.float32)


def activate(gate_up):
    return (jax.nn.silu(gate_up[0]) * gate_up[1]).astype(jnp.bfloat16)


def add_down(hidden, piece):
    return jnp.dot(hidden, piece, preferred_element_type=jnp.float32)


def shards(
    query_rows,
    key_rows,
    value_rows,
    doc_of_block,
    expert_ids,
    gate_weights,
    norm_gain,
    w_in,
    w_down,
):
    seq_count = lax.axis_size("seq")
    tok_count = query_rows.shape[1]
    blocks = doc_of_block[0]
    q_all, k_all, v_all = spread(seq_count, query_rows[0], key_rows[0], value_rows[0])
    team_first = lax.axis_index("seq") // TEAM * TEAM
    team_docs = lax.dynamic_slice(blocks, (team_first,), (TEAM,))
    same = team_docs[:, None] == blocks[None, :]
    number = jnp.arange(blocks.shape[0], dtype=jnp.int32)[None, :]
    low = jnp.min(jnp.where(same, number, blocks.shape[0]), axis=1)
    high = jnp.max(jnp.where(same, number, -1), axis=1)
    first = jnp.minimum(low, blocks.shape[0] - DOC_MOST)
    attended = attend(first, low, high, q_all, k_all, v_all)
    attn_float = collect(attended).astype(jnp.float32)
    mean_square = jnp.mean(attn_float * attn_float, axis=-1, keepdims=True)
    normed = (attn_float * lax.rsqrt(mean_square + EPS) * norm_gain).astype(jnp.bfloat16)
    chosen = expert_ids[0] == 0
    routed = jnp.any(chosen, axis=-1)
    gate_share = jnp.sum(jnp.where(chosen, gate_weights[0], 0.0), axis=-1)
    position = jnp.arange(tok_count, dtype=jnp.int32)
    earlier = (position[None, :] <= position[:, None]) & routed[None, :]
    slot_index = jnp.sum(earlier.astype(jnp.int32), axis=1) - 1
    onehot = (slot_index[None, :] == jnp.arange(CAP, dtype=jnp.int32)[:, None]) & routed[None, :]
    dispatched = jnp.dot(
        onehot.astype(jnp.bfloat16), normed, preferred_element_type=jnp.float32
    ).astype(jnp.bfloat16)
    w_in_pair = lax.all_gather(w_in, "grp", axis=1, tiled=True)
    w_down_pair = lax.all_gather(w_down, "grp", axis=0, tiled=True)
    gathered = lax.all_gather(dispatched, "seq", axis=0, tiled=True)
    gate_up = project_in(gathered, w_in_pair)
    hidden = activate(gate_up)
    terms = add_down(hidden, w_down_pair)
    returned = lax.psum_scatter(
        terms.astype(jnp.bfloat16), "seq", scatter_dimension=0, tiled=True
    )
    expert_out = lax.dot_general(
        onehot.astype(jnp.bfloat16),
        returned,
        (((0,), (0,)), ((), ())),
        preferred_element_type=jnp.float32,
    )
    layer_out = attn_float + gate_share[:, None] * expert_out
    return layer_out.astype(jnp.bfloat16)[None]


def solution(mesh):
    return jax.shard_map(
        shards,
        mesh=mesh,
        in_specs=(
            P("grp", "seq", None),
            P("grp", "seq", None),
            P("grp", "seq", None),
            P("grp", None),
            P("grp", "seq", None),
            P("grp", "seq", None),
            P(),
            P(None, ("seq", "grp"), None),
            P(("seq", "grp"), None),
        ),
        out_specs=P("grp", "seq", None),
        check_vma=False,
    )
```

time: 471 us -> 325 us (0.69); the launches traced: 464 us -> 324 us
  other arithmetic: 84.8 us -> 1.88 us
  Pallas kernels: 0 us -> 69.9 us
  local copies, waits for them, and re-layouts: 51.3 us -> 5.37 us
  waiting for transfers between devices: 241 us -> 212 us
  starting transfers between devices: 29.1 us -> 0.12 us
  matrix products: 43.6 us -> 21.9 us
    pallas_call x0 -> x3, Pallas kernels: none -> 69.9 us  [the longest x1 41.6 us: spread(): pl.pallas_call(functools.partial(spread_kernel, n), out_shape=(jax.ShapeD...]
    unnamed x4 -> x0, other arithmetic: 55.9 us -> none
    all_to_all x4 -> x0, waiting for transfers between devices: 35.9 us -> none  [the longest x1 22.7 us: shards(): lax.all_to_all(attended, 'seq', split_axis=1, concat_axis=2, tiled=True)]
    all_to_all x4 -> x0, starting transfers between devices: 28.5 us -> none  [the longest x1 8.53 us: shards(): lax.all_to_all(key_send, 'seq', split_axis=2, concat_axis=1, tiled=True)]
    broadcast_in_dim x5 -> x0, local copies, waits for them, and re-layouts: 28.2 us -> none  [the longest x1 11.7 us: attend(): return jnp.concatenate(outputs, axis=0)[None]]
    reduce_sum x6 -> x1, other arithmetic: 24.9 us -> 1.53 us  [shards(): mean_square = jnp.mean(attn_float * attn_float, axis=-1, keepdims=True)]
    dot_general x8 -> x0, matrix products: 21.1 us -> none  [the longest x4 10.6 us: attend(): jnp.einsum('qkgd,tkd->kgqt', query_tile, key_split, preferred_element_typ...]
    unnamed x46 -> x18, local copies, waits for them, and re-layouts: 15.4 us -> 5.3 us
  transfers between devices with their start and end apart: 8 -> 4, of which waited for: 5 -> 3; matrix products, arithmetic and copies ran while one was open for 31% -> 4% of each run, Pallas kernels for 0% -> 22%
where the time goes in v2:
time: 325 us; the launch traced here: 324 us
  waiting for transfers between devices  212 us (65%)
  Pallas kernels  69.9 us (22%)
  matrix products  21.9 us (7%)
  between operations  13.2 us (4%)
  local copies, waits for them, and re-layouts  5.37 us (2%)
    reduce_scatter x1, waiting for transfers between devices, shards(): lax.psum_scatter(terms.astype(jnp.bfloat16), 'seq', scatter_dimension=0,...  116 us
    all_gather x1, waiting for transfers between devices, shards(): gathered = lax.all_gather(dispatched, 'seq', axis=0, tiled=True)  91 us
    pallas_call x1, Pallas kernels, spread(): pl.pallas_call(functools.partial(spread_kernel, n), out_shape=(jax.ShapeD...  41.6 us
    pallas_call x1, Pallas kernels, collect(): pl.pallas_call(collect_kernel, out_shape=jax.ShapeDtypeStruct((attended.s...  14.2 us
    pallas_call x1, Pallas kernels, attend(): pl.pallas_call(attend_kernel, out_shape=jax.ShapeDtypeStruct(q.shape, jnp...  14.1 us
    dot_general x1, matrix products, project_in(): jnp.einsum('rd,khd->krh', gathered, piece, preferred_element_type=jnp.flo...  9.71 us
    dot_general x1, matrix products, add_down(): return jnp.dot(hidden, piece, preferred_element_type=jnp.float32)  7.32 us
  transfers between devices with their start and end apart: 4, of which 3 were waited for; matrix products, arithmetic and copies ran while one was open for 4% of the time, Pallas kernels for 22%

profile of v2, /device:TPU:0, one launch (start us, length us, event | category | flops | bytes accessed | tf_op | source)
XLA Modules:
  0.0 324.3 jit_solution(16272975629287827206)
XLA Ops:
  6.5 0.0 copy-start.7
  6.5 0.0 all-gather.6.cloned.1.call-start
  6.5 0.7 all-gather.6.cloned.1.call-update
  7.3 0.0 all-gather.4.cloned.1.call-start
  7.3 41.6 %spread.1 = (bf16[512,1024]{1,0:T(8,128)(2,1)}, bf16[2048,256]{1,0:T(8,128)(2,1)}, bf16[2048,256]{1,0:T(8,128)(2,1)}) custom-call(bf16[128,4096]{1,0:T(8,128)(2,1)} %bitcast.30, bf16[128,1024]{1,0:T(8,128)(2,1)} %bitcast.31, bf16[128,1024]{1,0:T(8,128)(2,1)} %bitcast.32), custom_call_target="tpu_custom_call" | custom-call | tf_op jit(solution)/shard_map/spread/pallas_call | solution.py:135
  49.0 0.0 copy-done.7
  49.0 0.1 dynamic-slice_bitcast_fusion
  49.0 0.2 fusion.27
  49.2 0.0 copy-start.1
  49.2 1.2 copy-done.1
  50.5 0.0 copy-start.2
  50.5 1.2 copy-done.2
  51.7 0.0 copy-start.3
  51.7 1.2 copy-done.3
  52.9 0.0 copy-start.5
  52.9 14.1 %attend.1.a_ref = bf16[512,1024]{1,0:T(8,128)(2,1)S(1)} custom-call(s32[4]{0:T(128)S(1)} %broadcast_minimum_fusion.start_ref, s32[4]{0:T(128)S(1)} %get-tuple-element.12.low_ref, s32[4]{0:T(128)S(1)} %get-tuple-element.11.high_ref, bf16[512,1024]{1,0:T(8,128)(2,1)S(1)} %copy-done.1, bf16[2048,256]{1,0:T(8,128)(2,1)S(1)} %copy-done.2, ...), custom_call_target="tpu_custom_call" | custom-call | tf_op jit(solution)/shard_map/attend/pallas_call | solution.py:177
  67.0 0.0 copy-start
  67.0 1.0 copy-done
  68.0 0.0 copy-start.8
  68.0 14.2 %collect.1 = bf16[128,4096]{1,0:T(8,128)(2,1)} custom-call(bf16[512,1024]{1,0:T(8,128)(2,1)} %copy-done), custom_call_target="tpu_custom_call" | custom-call | tf_op jit(solution)/shard_map/collect/pallas_call | solution.py:227
  82.2 0.0 copy-done.5
  82.2 0.1 convert_reduce_fusion
  82.3 1.5 fusion.5
  83.9 0.0 copy-done.8
  83.9 2.4 convolution_convert_fusion.1
  86.3 0.0 all-gather.4.cloned.1.call-update
  86.3 0.0 all-gather.8.cloned.1.call-start
  86.4 0.7 all-gather.8.cloned.1.call-update
  87.1 0.0 reduce-scatter.2.cloned.1.call-start
  87.1 0.0 all-gather.6.cloned.1.call-done
  87.2 91.0 %all-gather.4.cloned.1.call-done = bf16[640,4096]{1,0:T(8,128)(2,1)} async-done(((bf16[40,4096]{1,0:T(8,128)(2,1)}), bf16[640,4096]{1,0:T(8,128)(2,1)}) %all-gather.4.cloned.1.call-update) | async-done | bytes 5242896 | tf_op jit(solution)/shard_map/all_gather | solution.py:288
  178.1 9.7 %fusion.8 = f32[2,640,448]{1,2,0:T(8,128)S(1)} fusion(bf16[2,448,4096]{2,1,0:T(8,128)(2,1)} %all-gather.6.cloned.1.call-done, bf16[640,4096]{1,0:T(8,128)(2,1)} %all-gather.4.cloned.1.call-done), kind=kOutput, calls=%fused_computation.13 | convolution fusion | flops 4697620480 | bytes 14876672 | tf_op jit(solution)/shard_map/rd,khd->krh/dot_general | solution.py:239
  187.8 3.3 %all-gather.8.cloned.1.call-done = bf16[448,4096]{1,0:T(8,128)(2,1)} async-done(((bf16[224,4096]{1,0:T(8,128)(2,1)}), bf16[448,4096]{1,0:T(8,128)(2,1)}) %all-gather.8.cloned.1.call-update) | async-done | bytes 3670032 | tf_op jit(solution)/shard_map/all_gather | solution.py:287
  191.2 7.3 %convolution_convert_fusion = bf16[640,4096]{1,0:T(8,128)(2,1)} fusion(bf16[448,4096]{1,0:T(8,128)(2,1)} %all-gather.8.cloned.1.call-done, f32[2,640,448]{1,2,0:T(8,128)S(1)} %fusion.8), kind=kOutput, calls=%fused_computation | convolution fusion | flops 2353152000 | bytes 11206656 | tf_op jit(solution)/shard_map/dot_general | solution.py:247
  198.5 0.0 copy-start.6
  198.5 0.0 copy-start.4
  198.5 0.0 reduce-scatter.2.cloned.1.call-update
  198.5 0.7 copy-done.6
  199.2 116.1 %reduce-scatter.2.cloned.1.call-done = bf16[40,4096]{1,0:T(8,128)(2,1)} async-done(((bf16[640,4096]{1,0:T(8,128)(2,1)}), bf16[40,4096]{1,0:T(8,128)(2,1)}) %reduce-scatter.2.cloned.1.call-update) | async-done | bytes 327696 | tf_op jit(solution)/shard_map/reduce_scatter | solution.py:292
  315.3 0.0 copy-done.4
  315.3 2.4 fusion.4
  (5 shorter events, 0.1 us)
Async XLA Ops:
  6.5 42.4 %copy-start.7 = (s32[1,16]{1,0:T(1,128)S(1)}, s32[1,16]{1,0:T(1,128)}, u32[]{:S(2)}) copy-start(s32[1,16]{1,0:T(1,128)} %param.12) | copy-start | bytes 196
  6.5 80.6 %all-gather.6.cloned.1.call-start = ((), (), s32[]{:S(2)}) async-start(), calls=%async_computation.2 | async-start | bytes 11010048 | tf_op jit(solution)/shard_map/all_gather | solution.py:286
  7.3 170.9 %all-gather.4.cloned.1.call-start = ((), (), s32[]{:S(2)}) async-start(), calls=%async_computation.1 | async-start | bytes 5570560 | tf_op jit(solution)/shard_map/all_gather | solution.py:288
  49.2 1.2 copy-start.1
  50.5 1.2 copy-start.2
  51.7 1.2 copy-start.3
  52.9 29.3 %copy-start.5 = (s32[1,128,2]{1,2,0:T(2,128)S(1)}, s32[1,128,2]{1,2,0:T(2,128)}, u32[]{:S(2)}) copy-start(s32[1,128,2]{1,2,0:T(2,128)} %param.13) | copy-start | bytes 3076
  67.0 1.0 copy-start
  68.0 15.9 %copy-start.8 = (f32[4096]{0:T(1024)S(1)}, f32[4096]{0:T(1024)}, u32[]{:S(2)}) copy-start(f32[4096]{0:T(1024)} %param.15) | copy-start | bytes 49156
  86.3 104.8 %all-gather.8.cloned.1.call-start = ((), (), s32[]{:S(2)}) async-start(), calls=%async_computation.3 | async-start | bytes 5505024 | tf_op jit(solution)/shard_map/all_gather | solution.py:287
  87.1 228.2 %reduce-scatter.2.cloned.1.call-start = ((), (), s32[]{:S(2)}) async-start(), calls=%async_computation.4 | async-start | bytes 5570560 | tf_op jit(solution)/shard_map/reduce_scatter | solution.py:292
  198.5 0.7 copy-start.6
  198.5 116.8 %copy-start.4 = (bf16[128,4096]{1,0:T(8,128)(2,1)S(1)}, bf16[128,4096]{1,0:T(8,128)(2,1)}, u32[]{:S(2)}) copy-start(bf16[128,4096]{1,0:T(8,128)(2,1)} %collect.1) | copy-start | bytes 3145732
Sparse Core Ops, SparseCore 0:
  8.9 20.9 all-gather.5
  86.5 91.6 all-gather.3
  179.7 11.4 all-gather.7
  198.6 116.6 reduce-scatter.1

commit v3 on v2

--- a/solution.py
+++ b/solution.py
@@ -245,6 +245,209 @@
 
 def add_down(hidden, piece):
     return jnp.dot(hidden, piece, preferred_element_type=jnp.float32)
+
+
+def places(n):
+    me = lax.axis_index("seq")
+    team, j = me // TEAM, lax.rem(me, TEAM)
+    near = j + 1 - 2 * lax.rem(j, 2)
+    over = j + 2 - 4 * (j // 2)
+    return team, j, near, over, n // TEAM
+
+
+def greet_cross(n):
+    team, j, near, over, teams = places(n)
+    barrier = pltpu.get_barrier_semaphore()
+    others = [team * TEAM + near, team * TEAM + over]
+    others += [lax.rem(team + k, teams) * TEAM + j for k in range(1, teams)]
+    for other in others:
+        pl.semaphore_signal(
+            barrier, inc=1, device_id={"seq": other}, device_id_type=pl.DeviceIdType.MESH
+        )
+    pl.semaphore_wait(barrier, len(others))
+
+
+def push(src, dst, send, recv, to):
+    return pltpu.make_async_remote_copy(
+        src_ref=src,
+        dst_ref=dst,
+        send_sem=send,
+        recv_sem=recv,
+        device_id={"seq": to},
+        device_id_type=pl.DeviceIdType.MESH,
+    )
+
+
+def gather_kernel(n, x_ref, o_ref, cs, cr, ps, pr, own):
+    team, j, near, over, teams = places(n)
+    half = x_ref.shape[1] // 2
+    greet_cross(n)
+
+    def piece(k, column):
+        return lax.rem(team + teams - k, teams) * TEAM + column
+
+    def along(k):
+        return push(
+            x_ref,
+            o_ref.at[team * TEAM + j],
+            cs.at[k],
+            cr.at[k],
+            lax.rem(team + k, teams) * TEAM + j,
+        )
+
+    def across(k, way, to):
+        index = piece(k, j)
+        src = x_ref if k == 0 else o_ref.at[index]
+        return push(src, o_ref.at[index], ps.at[k, way], pr.at[k, way], team * TEAM + to)
+
+    def relay(k, way, source, part, to):
+        view = o_ref.at[piece(k, source), :, pl.ds(part * half, half)]
+        return push(view, view, ps.at[k, way], pr.at[k, way], team * TEAM + to)
+
+    def fulls(k):
+        return across(k, 0, near), across(k, 1, over)
+
+    def relays(k):
+        return relay(k, 2, near, 0, over), relay(k, 3, over, 1, near)
+
+    for k in range(1, teams):
+        along(k).start()
+    for copy in fulls(0):
+        copy.start()
+    mine = pltpu.make_async_copy(x_ref, o_ref.at[team * TEAM + j], own.at[0])
+    mine.start()
+    for k in range(teams):
+        if k + 1 < teams:
+            along(k + 1).wait_recv()
+            for copy in fulls(k + 1):
+                copy.start()
+        for full, passed in zip(fulls(k), relays(k)):
+            full.wait_recv()
+            passed.start()
+    for k in range(teams):
+        for copy in relays(k):
+            copy.wait()
+        for copy in fulls(k):
+            copy.wait_send()
+        if k:
+            along(k).wait_send()
+    mine.wait()
+
+
+def gather_rows(n, rows):
+    any_spec = pl.BlockSpec(memory_space=pl.ANY)
+    dma = pltpu.SemaphoreType.DMA
+    teams = n // TEAM
+    return pl.pallas_call(
+        functools.partial(gather_kernel, n),
+        out_shape=jax.ShapeDtypeStruct((n,) + rows.shape, jnp.bfloat16),
+        in_specs=[any_spec],
+        out_specs=any_spec,
+        scratch_shapes=[dma((teams,))] * 2 + [dma((teams, 4))] * 2 + [dma((1,))],
+        compiler_params=pltpu.CompilerParams(collective_id=2, has_side_effects=True),
+        name="gather_rows",
+    )(rows)
+
+
+def reduce_kernel(n, t_ref, o_ref, *scratch):
+    far_a, far_b, add_a, add_b, from_near, from_over, plane, arrived, ps, pr, cs, cr = scratch
+    team, j, near, over, teams = places(n)
+    half = t_ref.shape[2] // 2
+    first, second = pl.ds(0, half), pl.ds(half, half)
+    f32 = jnp.float32
+    greet_cross(n)
+
+    def index(k, column):
+        return lax.rem(team + k, teams) * TEAM + column
+
+    def hop(k, way, src, dst, to):
+        return push(src, dst, ps.at[k, way], pr.at[k, way], team * TEAM + to)
+
+    def early(k):
+        across = TEAM - 1 - j
+        return (
+            hop(k, 0, t_ref.at[index(k, across), :, first], far_a.at[k], near),
+            hop(k, 1, t_ref.at[index(k, across), :, second], far_b.at[k], over),
+            hop(k, 2, t_ref.at[index(k, near), :, first], from_near.at[k, 0], near),
+            hop(k, 3, t_ref.at[index(k, over), :, second], from_over.at[k, 1], over),
+        )
+
+    def late(k):
+        return (
+            hop(k, 4, add_a.at[k], from_over.at[k, 0], over),
+            hop(k, 5, add_b.at[k], from_near.at[k, 1], near),
+        )
+
+    def along(k):
+        return push(plane.at[k], arrived.at[k], cs.at[k], cr.at[k], index(k, j))
+
+    def finish(k):
+        for copy in early(k)[2:] + late(k):
+            copy.wait_recv()
+        parts = []
+        for part, cut in ((0, first), (1, second)):
+            parts.append(
+                t_ref[index(k, j), :, cut].astype(f32)
+                + from_near[k, part].astype(f32)
+                + from_over[k, part].astype(f32)
+            )
+        return parts
+
+    order = list(range(teams - 1, -1, -1))
+    for k in order:
+        for copy in early(k):
+            copy.start()
+    for k in order:
+        to_near, to_over = early(k)[:2]
+        pass_a, pass_b = late(k)
+        to_near.wait_recv()
+        add_a[k] = (far_a[k].astype(f32) + t_ref[index(k, over), :, first].astype(f32)).astype(
+            jnp.bfloat16
+        )
+        pass_a.start()
+        to_over.wait_recv()
+        add_b[k] = (far_b[k].astype(f32) + t_ref[index(k, near), :, second].astype(f32)).astype(
+            jnp.bfloat16
+        )
+        pass_b.start()
+        if k + 1 < teams:
+            low_sum, high_sum = finish(k + 1)
+            plane[k + 1, :, first] = low_sum.astype(jnp.bfloat16)
+            plane[k + 1, :, second] = high_sum.astype(jnp.bfloat16)
+            along(k + 1).start()
+    for k in range(1, teams):
+        along(k).wait()
+    for cut, total in zip((first, second), finish(0)):
+        for k in range(1, teams):
+            total = total + arrived[k, :, cut].astype(f32)
+        o_ref[:, cut] = total.astype(jnp.bfloat16)
+    for k in range(teams):
+        for copy in early(k) + late(k):
+            copy.wait_send()
+
+
+def reduce_rows(n, terms):
+    dma = pltpu.SemaphoreType.DMA
+    teams = n // TEAM
+    rows, width = terms.shape[1:]
+    halves = pltpu.VMEM((teams, rows, width // 2), jnp.bfloat16)
+    pairs = pltpu.VMEM((teams, 2, rows, width // 2), jnp.bfloat16)
+    wholes = pltpu.VMEM((teams, rows, width), jnp.bfloat16)
+    return pl.pallas_call(
+        functools.partial(reduce_kernel, n),
+        out_shape=jax.ShapeDtypeStruct((rows, width), jnp.bfloat16),
+        in_specs=[pl.BlockSpec(memory_space=pltpu.VMEM)],
+        out_specs=pl.BlockSpec(memory_space=pltpu.VMEM),
+        scratch_shapes=[halves] * 4
+        + [pairs] * 2
+        + [wholes] * 2
+        + [dma((teams, 6))] * 2
+        + [dma((teams,))] * 2,
+        compiler_params=pltpu.CompilerParams(
+            collective_id=3, has_side_effects=True, vmem_limit_bytes=40 * 2**20
+        ),
+        name="reduce_rows",
+    )(terms)
 
 
 def shards(
@@ -285,12 +488,12 @@
     ).astype(jnp.bfloat16)
     w_in_pair = lax.all_gather(w_in, "grp", axis=1, tiled=True)
     w_down_pair = lax.all_gather(w_down, "grp", axis=0, tiled=True)
-    gathered = lax.all_gather(dispatched, "seq", axis=0, tiled=True)
+    gathered = gather_rows(seq_count, dispatched).reshape(-1, dispatched.shape[1])
     gate_up = project_in(gathered, w_in_pair)
     hidden = activate(gate_up)
     terms = add_down(hidden, w_down_pair)
-    returned = lax.psum_scatter(
-        terms.astype(jnp.bfloat16), "seq", scatter_dimension=0, tiled=True
+    returned = reduce_rows(
+        seq_count, terms.astype(jnp.bfloat16).reshape((seq_count,) + dispatched.shape)
     )
     expert_out = lax.dot_general(
         onehot.astype(jnp.bfloat16),

time: 325 us -> 235 us (0.72)
  waiting for transfers between devices: 212 us -> 1.44 us
  Pallas kernels: 69.9 us -> 194 us
  matrix products: 21.9 us -> 18.6 us
    pallas_call x0 -> x2, Pallas kernels: none -> 124 us  [the longest x1 65 us: reduce_rows(): pl.pallas_call(functools.partial(reduce_kernel, n), out_shape=jax.ShapeDt...]
    reduce_scatter x1 -> x0, waiting for transfers between devices: 116 us -> none  [shards(): lax.psum_scatter(terms.astype(jnp.bfloat16), 'seq', scatter_dimension=0,...]
    all_gather x1 -> x0, waiting for transfers between devices: 91 us -> none  [shards(): gathered = lax.all_gather(dispatched, 'seq', axis=0, tiled=True)]
    all_gather x1, waiting for transfers between devices: 3.31 us -> 0.02 us  [shards(): w_down_pair = lax.all_gather(w_down, 'grp', axis=0, tiled=True)]
  transfers between devices with their start and end apart: 4 -> 2, of which waited for: 3 -> 0; matrix products, arithmetic and copies ran while one was open for 4% -> 6% of each run, Pallas kernels for 22% -> 55%
where the time goes in v3:
time: 235 us; the launch traced here: 234 us
  Pallas kernels  194 us (83%)
  matrix products  18.6 us (8%)
  between operations  13.6 us (6%)
  local copies, waits for them, and re-layouts  4.73 us (2%)
    pallas_call x1, Pallas kernels, reduce_rows(): pl.pallas_call(functools.partial(reduce_kernel, n), out_shape=jax.ShapeDt...  65 us
    pallas_call x1, Pallas kernels, gather_rows(): pl.pallas_call(functools.partial(gather_kernel, n), out_shape=jax.ShapeDt...  59.2 us
    pallas_call x1, Pallas kernels, spread(): pl.pallas_call(functools.partial(spread_kernel, n), out_shape=(jax.ShapeD...  41.6 us
    pallas_call x1, Pallas kernels, collect(): pl.pallas_call(collect_kernel, out_shape=jax.ShapeDtypeStruct((attended.s...  14.2 us
    pallas_call x1, Pallas kernels, attend(): pl.pallas_call(attend_kernel, out_shape=jax.ShapeDtypeStruct(q.shape, jnp...  14.1 us
    dot_general x1, matrix products, project_in(): jnp.einsum('rd,khd->krh', gathered, piece, preferred_element_type=jnp.flo...  9.75 us
    dot_general x1, matrix products, add_down(): return jnp.dot(hidden, piece, preferred_element_type=jnp.float32)  5 us
  transfers between devices with their start and end apart: 2, of which 0 were waited for; matrix products, arithmetic and copies ran while one was open for 6% of the time, Pallas kernels for 55%

profile of v3, /device:TPU:0, one launch (start us, length us, event | category | flops | bytes accessed | tf_op | source)
XLA Modules:
  0.0 234.4 jit_solution(12436023652327248472)
XLA Ops:
  6.5 0.0 all-gather.3.cloned.1.call-start
  6.5 0.7 all-gather.3.cloned.1.call-update
  7.3 0.0 copy-start.7
  7.3 0.0 all-gather.5.cloned.1.call-start
  7.3 0.7 all-gather.5.cloned.1.call-update
  8.0 41.6 %spread.1 = (bf16[512,1024]{1,0:T(8,128)(2,1)}, bf16[2048,256]{1,0:T(8,128)(2,1)}, bf16[2048,256]{1,0:T(8,128)(2,1)}) custom-call(bf16[128,4096]{1,0:T(8,128)(2,1)} %bitcast.32, bf16[128,1024]{1,0:T(8,128)(2,1)} %bitcast.33, bf16[128,1024]{1,0:T(8,128)(2,1)} %bitcast.34), custom_call_target="tpu_custom_call" | custom-call | tf_op jit(solution)/shard_map/spread/pallas_call | solution.py:135
  49.7 0.0 copy-done.7
  49.7 0.1 dynamic-slice_bitcast_fusion
  49.8 0.2 fusion.22
  49.9 0.0 copy-start.1
  50.0 1.2 copy-done.1
  51.2 0.0 copy-start.2
  51.2 1.2 copy-done.2
  52.4 0.0 copy-start.3
  52.4 1.2 copy-done.3
  53.6 0.0 copy-start.5
  53.6 14.1 %attend.1.a_ref = bf16[512,1024]{1,0:T(8,128)(2,1)S(1)} custom-call(s32[4]{0:T(128)S(1)} %broadcast_minimum_fusion.start_ref, s32[4]{0:T(128)S(1)} %get-tuple-element.12.low_ref, s32[4]{0:T(128)S(1)} %get-tuple-element.11.high_ref, bf16[512,1024]{1,0:T(8,128)(2,1)S(1)} %copy-done.1, bf16[2048,256]{1,0:T(8,128)(2,1)S(1)} %copy-done.2, ...), custom_call_target="tpu_custom_call" | custom-call | tf_op jit(solution)/shard_map/attend/pallas_call | solution.py:177
  67.7 0.0 copy-start
  67.7 1.0 copy-done
  68.7 0.0 copy-start.8
  68.7 14.2 %collect.1 = bf16[128,4096]{1,0:T(8,128)(2,1)} custom-call(bf16[512,1024]{1,0:T(8,128)(2,1)} %copy-done), custom_call_target="tpu_custom_call" | custom-call | tf_op jit(solution)/shard_map/collect/pallas_call | solution.py:227
  82.9 0.0 copy-done.5
  82.9 0.1 convert_reduce_fusion
  83.0 1.5 fusion.3
  84.6 0.0 copy-done.8
  84.6 2.4 %convolution_convert_fusion.1.x_ref = bf16[40,4096]{1,0:T(8,128)(2,1)} fusion(bf16[128,4096]{1,0:T(8,128)(2,1)} %collect.1, f32[4096]{0:T(1024)S(1)} %copy-done.8, f32[128]{0:T(128)S(1)} %add_rsqrt_fusion, s32[128]{0:T(128)S(1)} %broadcast_add_fusion, pred[128]{0:T(512)(128)(4,1)S(1)} %fusion.23), kind=kOutput, calls=%fused_computation.5 | convolution fusion | flops 44214272 | bytes 1393792 | tf_op jit(solution)/shard_map/dot_general | solution.py:486
  87.0 0.0 copy-start.6
  87.0 59.2 %gather_rows.1 = bf16[16,40,4096]{2,1,0:T(8,128)(2,1)} custom-call(bf16[40,4096]{1,0:T(8,128)(2,1)} %convolution_convert_fusion.1.x_ref), custom_call_target="tpu_custom_call" | custom-call | tf_op jit(solution)/shard_map/gather_rows/pallas_call | solution.py:341
  146.2 0.0 copy-done.6
  146.3 0.0 all-gather.3.cloned.1.call-done
  146.3 9.7 %convolution_bitcast_fusion = f32[2,640,448]{1,2,0:T(8,128)S(1)} fusion(bf16[640,4096,1]{1,0,2:T(8,128)(2,1)} %bitcast.31, bf16[2,448,4096]{2,1,0:T(8,128)(2,1)} %all-gather.3.cloned.1.call-done), kind=kOutput, calls=%fused_computation.11 | convolution fusion | flops 4697620480 | bytes 14876672 | tf_op jit(solution)/shard_map/rd,khd->krh/dot_general | solution.py:239
  156.0 0.0 all-gather.5.cloned.1.call-done
  156.1 5.0 %convolution_convert_fusion = bf16[640,4096]{1,0:T(8,128)(2,1)S(1)} fusion(bf16[448,4096]{1,0:T(8,128)(2,1)} %all-gather.5.cloned.1.call-done, f32[2,640,448]{1,2,0:T(8,128)S(1)} %convolution_bitcast_fusion), kind=kOutput, calls=%fused_computation | convolution fusion | flops 2353152000 | bytes 11206656 | tf_op jit(solution)/shard_map/dot_general | solution.py:247
  161.1 0.0 copy-start.4
  161.1 65.0 %reduce_rows.1 = bf16[40,4096]{1,0:T(8,128)(2,1)S(1)} custom-call(bf16[16,40,4096]{2,1,0:T(8,128)(2,1)S(1)} %bitcast.30), custom_call_target="tpu_custom_call" | custom-call | tf_op jit(solution)/shard_map/reduce_rows/pallas_call | solution.py:436
  226.1 0.0 copy-done.4
  226.1 1.5 fusion.2
  (5 shorter events, 0.1 us)
Async XLA Ops:
  6.5 139.7 %all-gather.3.cloned.1.call-start = ((), (), s32[]{:S(2)}) async-start(), calls=%async_computation | async-start | bytes 11010048 | tf_op jit(solution)/shard_map/all_gather | solution.py:489
  7.3 42.4 %copy-start.7 = (s32[1,16]{1,0:T(1,128)S(1)}, s32[1,16]{1,0:T(1,128)}, u32[]{:S(2)}) copy-start(s32[1,16]{1,0:T(1,128)} %param.12) | copy-start | bytes 196
  7.3 148.8 %all-gather.5.cloned.1.call-start = ((), (), s32[]{:S(2)}) async-start(), calls=%async_computation.1 | async-start | bytes 5505024 | tf_op jit(solution)/shard_map/all_gather | solution.py:490
  49.9 1.2 copy-start.1
  51.2 1.2 copy-start.2
  52.4 1.2 copy-start.3
  53.6 29.3 %copy-start.5 = (s32[1,128,2]{1,2,0:T(2,128)S(1)}, s32[1,128,2]{1,2,0:T(2,128)}, u32[]{:S(2)}) copy-start(s32[1,128,2]{1,2,0:T(2,128)} %param.13) | copy-start | bytes 3076
  67.7 1.0 copy-start
  68.7 15.9 %copy-start.8 = (f32[4096]{0:T(1024)S(1)}, f32[4096]{0:T(1024)}, u32[]{:S(2)}) copy-start(f32[4096]{0:T(1024)} %param.15) | copy-start | bytes 49156
  87.0 59.2 %copy-start.6 = (f32[1,128,2]{1,2,0:T(2,128)S(1)}, f32[1,128,2]{1,2,0:T(2,128)}, u32[]{:S(2)}) copy-start(f32[1,128,2]{1,2,0:T(2,128)} %param.14) | copy-start | bytes 3076
  161.1 65.1 %copy-start.4 = (bf16[128,4096]{1,0:T(8,128)(2,1)S(1)}, bf16[128,4096]{1,0:T(8,128)(2,1)}, u32[]{:S(2)}) copy-start(bf16[128,4096]{1,0:T(8,128)(2,1)} %collect.1) | copy-start | bytes 3145732
Sparse Core Ops, SparseCore 0:
  8.9 20.9 all-gather.2
  31.5 14.0 all-gather.4
